TPU v7x, 256 devices: a whole 4x4x8 slice. The times are simulated.
256 devices in a mesh: dp: 4 (over x_hi, core), ctx: 16 (over z, x_lo), tensor: 4 (over y).
Axes of the slice: x: 4 (x_hi: 2, x_lo: 2; x = x_hi * 2 + x_lo), y: 4, z: 8, core: 2. Of those that a mesh axis runs over, the one named last changes fastest.
Arguments:
- query_latent: bfloat16 [4, 8192, 1536], P('dp', 'ctx'), may hold values from -6 to 6
- shared_latent: bfloat16 [4, 8192, 512], P('dp', 'ctx'), may hold values from -6 to 6
- rope_keys: bfloat16 [4, 8192, 64], P('dp', 'ctx'), may hold values from -6 to 6
- block_order: int32 [4, 16], replicated, may hold values from 0 to 15, each once within a row
- query_weight: bfloat16 [1536, 12288], P(('dp', 'ctx'), 'tensor'), as said below
- key_weight: bfloat16 [512, 8192], P(('dp', 'ctx'), 'tensor'), may hold values from -0.25 to 0.25
- value_weight: bfloat16 [512, 8192], P(('dp', 'ctx'), 'tensor'), may hold values from -0.25 to 0.25
Outputs:
- attended: bfloat16 [4, 8192, 8192], P('dp', 'ctx', 'tensor')
- logit_max: float32 [64], P('tensor')
- clipped_query_weight: bfloat16 [1536, 12288], P(('dp', 'ctx'), 'tensor')
- clipped_key_weight: bfloat16 [512, 8192], P(('dp', 'ctx'), 'tensor')
Inputs may be any that keep to these rules, and one draw needn't show every extreme that they name: `block_order`: each row is a permutation: every block of a sequence is held by exactly one ctx index. `query_weight`: entries of each head's columns have a head-dependent spread.
All inputs are finite; a program needn't handle non-finite values.
Results may differ from a plain program's by a relative error of at most 0.012.
The roundings to bfloat16 on the way count: a program that leaves them out, or rounds other values in their place, can miss the bound.
Values may be sent and summed in bfloat16 or wider, within the bound.
No kernel may reach another device: no remote copies, remote signals or barrier semaphores. Data moves between devices by JAX's collectives and lax.ppermute only.
A program may use at most 128 MiB of HBM per device.

v0:
```python
import functools
import math

import jax
import jax.numpy as jnp
from jax import lax
from jax.experimental import pallas as pl
from jax.experimental.pallas import tpu as pltpu
from jax.sharding import Mesh
from jax.sharding import PartitionSpec as P

QK_NOPE = 128
QK_ROPE = 64
V_DIM = 128
TAU = 100
HEAD = QK_NOPE + QK_ROPE
SCALE = 1.0 / math.sqrt(HEAD)
SCALE2 = SCALE * math.log2(math.e)
FAR = 1e30

GROUP = ("xh", "core", "z", "xl")
X = ("xh", "xl")
TOK = 512
HALF = TOK // 2
GROUPS_A = (2,) * 5
GROUPS_B = (2,) * 3
HEADS_A = sum(GROUPS_A)
HEADS_B = sum(GROUPS_B)
WIDE = 3 * HEAD + QK_NOPE + V_DIM
MIB = 1024 * 1024
VMEM = pl.BlockSpec(memory_space=pltpu.VMEM)
SMEM = pl.BlockSpec(memory_space=pltpu.SMEM)
ANY = pl.BlockSpec(memory_space=pl.ANY)


def in_hbm(array):
    return pltpu.with_memory_space_constraint(array, pltpu.HBM)


def whole(shape):
    return pl.BlockSpec(shape, lambda p: (0,) * len(shape))


def dot_f32(a, b):
    return jnp.dot(a, b, preferred_element_type=jnp.float32)


def dot_t(a, b):
    return lax.dot_general(a, b, (((1,), (1,)), ((), ())), preferred_element_type=jnp.float32)


def attend_some(heads, seen, x_ref, lat_ref, rope_ref, weight, out_ref, peak_ref):
    query = [dot_f32(x_ref[j], weight(j * heads * HEAD, heads * HEAD)) for j in range(3)]
    query = functools.reduce(jnp.add, query).astype(jnp.bfloat16)
    at = 3 * heads * HEAD
    keys = dot_f32(lat_ref[...], weight(at, heads * QK_NOPE)).astype(jnp.bfloat16)
    values = dot_f32(lat_ref[...], weight(at + heads * QK_NOPE, heads * V_DIM)).astype(jnp.bfloat16)
    rope = rope_ref[...]
    row = lax.broadcasted_iota(jnp.int32, (HALF, HALF), 0)
    col = lax.broadcasted_iota(jnp.int32, (HALF, HALF), 1)
    diagonal = col <= row
    ones = (lax.broadcasted_iota(jnp.int32, (2 * TOK, V_DIM), 1) == 0).astype(jnp.bfloat16)

    def logits_of(head, part):
        q_part = query[part * HALF : (part + 1) * HALF, head * HEAD : (head + 1) * HEAD]
        key_head = jnp.concatenate([keys[:, head * QK_NOPE : (head + 1) * QK_NOPE], rope], axis=1)
        spans = [(0, HALF, "all")] if part == 1 else []
        spans += [(part * HALF, HALF, "diag"), (TOK, TOK, "prev")]
        logits = []
        for start, size, kind in spans:
            s = dot_t(q_part, key_head[start : start + size])
            logits.append(jnp.where(diagonal, s, -jnp.inf) if kind == "diag" else s)
        return spans, logits

    def finish(head, part, spans, logits):
        value_head = jnp.concatenate([values[:, head * V_DIM : (head + 1) * V_DIM], ones], axis=1)
        peak = functools.reduce(jnp.maximum, [jnp.max(s, axis=1, keepdims=True) for s in logits[:-1]])
        prev_peak = jnp.max(logits[-1], axis=1, keepdims=True)
        peak = jnp.where(seen, jnp.maximum(peak, prev_peak), peak)
        shift = peak * SCALE2
        shift_prev = jnp.where(seen, shift, FAR)
        result = None
        for s, (start, size, kind) in zip(logits, spans):
            expo = jnp.exp2(s * SCALE2 - (shift_prev if kind == "prev" else shift))
            term = dot_f32(expo.astype(jnp.bfloat16), value_head[start : start + size])
            result = term if result is None else result + term
        result = result[:, :V_DIM] * (1.0 / result[:, V_DIM : V_DIM + 1])
        out_ref[part * HALF : (part + 1) * HALF, head * V_DIM : (head + 1) * V_DIM] = result.astype(jnp.bfloat16)
        return jnp.max(peak)

    order = [(head, part) for head in range(heads) for part in range(2)]
    peaks = []
    current = logits_of(*order[0])
    for i, (head, part) in enumerate(order):
        following = logits_of(*order[i + 1]) if i + 1 < len(order) else None
        peaks.append(finish(head, part, *current))
        current = following
    for head in range(heads):
        top = jnp.maximum(peaks[2 * head], peaks[2 * head + 1]) * SCALE
        peak_ref[head : head + 1, :] = jnp.broadcast_to(top, (1, 128))


def from_gathered(place_ref, pieces):
    return [(pieces[0], pl.ds(0, TOK))]


def from_ring(place_ref, pieces):
    me, core = place_ref[1], place_ref[2]
    made = []
    for side in range(2):
        owner = core if side == 0 else 1 - core
        for piece, distance, first in zip(pieces[5 * side : 5 * side + 5], (0, 3, 1, 2, 2), (0, 0, 0, 0, 32)):
            block = lax.rem(me + distance, 4) * 2 + owner
            made.append((piece, pl.ds(pl.multiple_of(block * 64 + first, 32), piece.shape[0])))
    return made


def attend_kernel(rows_of, heads, steps, count, away, place_ref, x_ref, lat_ref, rope_ref, *rest):
    pieces = rest[:count]
    out_ref, peak_ref, w_ref, sems, own_sems, *own = rest[-8 if away else -5 :]
    rows = rows_of(place_ref, pieces)
    loads = [pltpu.make_async_copy(*pair, own_sems.at[i]) for i, pair in enumerate(zip((x_ref, lat_ref, rope_ref), own))]
    if away:
        x_ref, lat_ref, rope_ref = own
    step = pl.program_id(0)
    slot = lax.rem(step, 2)
    wide = heads * WIDE

    def copies(step, slot):
        columns = pl.ds(pl.multiple_of(step * wide, 128), wide)
        return [
            pltpu.make_async_copy(piece.at[:, columns], w_ref.at[slot, where], sems.at[slot, i])
            for i, (piece, where) in enumerate(rows)
        ]

    @pl.when(step == 0)
    def _():
        for copy in [*loads, *copies(0, 0)]:
            copy.start()
        for load in loads:
            load.wait()

    for copy in copies(step, slot):
        copy.wait()

    @pl.when(step + 1 < steps)
    def _():
        for copy in copies(step + 1, 1 - slot):
            copy.start()

    weight = lambda at, width: w_ref[slot, :, at : at + width]
    attend_some(heads, place_ref[0] > 0, x_ref, lat_ref, rope_ref, weight, out_ref, peak_ref.at[0])


def attend(rows_of, groups, first, name, place, x, latents, rope, pieces, before=()):
    heads, steps, count, away = groups[0], len(groups), len(pieces), bool(before)
    own = (x, latents, rope)
    return pl.pallas_call(
        functools.partial(attend_kernel, rows_of, heads, steps, count, away),
        grid=(steps,),
        in_specs=[SMEM] + [ANY if away else VMEM] * 3 + [ANY] * (count + len(before)),
        out_specs=[
            pl.BlockSpec((TOK, heads * V_DIM), lambda p: (0, first // heads + p)),
            pl.BlockSpec((1, 8, 128), lambda p: (p, 0, 0)),
        ],
        out_shape=[
            jax.ShapeDtypeStruct((TOK, (HEADS_A + HEADS_B) * V_DIM), jnp.bfloat16),
            jax.ShapeDtypeStruct((steps, 8, 128), jnp.float32),
        ],
        input_output_aliases={4 + count: 0} if before else {},
        scratch_shapes=[
            pltpu.VMEM((2, TOK, heads * WIDE), jnp.bfloat16),
            pltpu.SemaphoreType.DMA((2, count)),
            pltpu.SemaphoreType.DMA((3,)),
        ]
        + [pltpu.VMEM(a.shape, a.dtype) for a in (own if away else ())],
        compiler_params=pltpu.CompilerParams(vmem_limit_bytes=20 * MIB),
        cost_estimate=pl.CostEstimate(
            flops=900_000_000 * heads * steps,
            bytes_accessed=1_000_000 * heads * steps,
            transcendentals=500_000 * heads * steps,
        ),
        name=name,
    )(place, *[in_hbm(a) if away else a for a in own], *pieces, *before)


def pack_kernel(q_ref, k_ref, v_ref, a_ref, b_ref):
    head = 0
    for groups, ref in ((GROUPS_A, a_ref), (GROUPS_B, b_ref)):
        at = 0
        for heads in groups:
            for j in range(3):
                columns = slice(head * HEAD, (head + heads) * HEAD)
                ref[:, at : at + heads * HEAD] = q_ref[8 * j : 8 * j + 8, columns]
                at += heads * HEAD
            for source in (k_ref, v_ref):
                ref[:, at : at + heads * QK_NOPE] = source[:, head * QK_NOPE : (head + heads) * QK_NOPE]
                at += heads * QK_NOPE
            head += heads


def pack(*weights):
    shapes = [jax.ShapeDtypeStruct((8, heads * WIDE), jnp.bfloat16) for heads in (HEADS_A, HEADS_B)]
    return pl.pallas_call(
        pack_kernel,
        grid=(1,),
        in_specs=[whole(a.shape) for a in weights],
        out_specs=[whole(a.shape) for a in shapes],
        out_shape=shapes,
        compiler_params=pltpu.CompilerParams(vmem_limit_bytes=8 * MIB),
        name="pack",
    )(*[in_hbm(a) for a in weights])


def order_kernel(offsets, me_ref, *refs):
    pieces, out_ref = refs[:-1], refs[-1]
    count = len(pieces)
    for offset, piece in zip(offsets, pieces):
        out_ref[lax.rem(me_ref[0] + offset % count, count)] = piece[...]


def in_order(me, offsets, pieces):
    rows, columns = pieces[0].shape
    count = len(pieces)
    return pl.pallas_call(
        functools.partial(order_kernel, offsets),
        in_specs=[SMEM] + [VMEM] * count,
        out_specs=VMEM,
        out_shape=jax.ShapeDtypeStruct((count, rows, columns), jnp.bfloat16),
        compiler_params=pltpu.CompilerParams(vmem_limit_bytes=4 * MIB),
        name="in_order",
    )(me.reshape(1), *pieces).reshape(count * rows, columns)


def halves_kernel(before_ref, after_ref, low_ref, high_ref):
    low_ref[...] = before_ref[:32]
    high_ref[...] = after_ref[32:]


def halves(before, after):
    shape = jax.ShapeDtypeStruct((32, before.shape[1]), before.dtype)
    return pl.pallas_call(
        halves_kernel,
        in_specs=[VMEM] * 2,
        out_specs=[VMEM] * 2,
        out_shape=[shape, shape],
        compiler_params=pltpu.CompilerParams(vmem_limit_bytes=4 * MIB),
        name="halves",
    )(before, after)


def one_hot(source, first):
    at = lax.broadcasted_iota(jnp.int32, (128, source.shape[1]), 0) + first
    return jnp.where(at == source, 1.0, 0.0).astype(jnp.bfloat16)


def picked(rows, tiles, source):
    left = jnp.concatenate([rows(tile) for tile in tiles], axis=1)
    right = jnp.concatenate([one_hot(source, tile * 128) for tile in tiles], axis=0)
    return dot_f32(left, right).astype(jnp.bfloat16)


def late_source(c, tile, strip):
    z, core, xh, xl, r = 2 * tile + ((c >> 6) & 1), (c >> 5) & 1, (c >> 4) & 1, (c >> 3) & 1, c & 7
    return ((xh * 2 + core) * 16 + z * 2 + xl) * strip + r


def early_source(c, tile, strip):
    core, z, r = (c >> 6) & 1, (c >> 3) & 7, c & 7
    return ((tile // 2 * 2 + core) * 16 + z * 2 + tile % 2) * strip + r


def order_query_kernel(x_ref, late_ref, early_ref):
    column = lax.broadcasted_iota(jnp.int32, (1, 384), 1)
    c, j = column & 127, column >> 7
    rows = lambda tile: x_ref[:, tile * 128 : (tile + 1) * 128]
    for tile in range(4):
        low, high = 96 * tile // 128, (96 * tile + 95) // 128
        near = [3 * block + part for block in range(4) for part in range(low, high + 1)]
        late = picked(rows, near, late_source(c, tile, 24) + 8 * j)
        near = [3 * (tile // 2 * 2 + core) + part for core in range(2) for part in range(3)]
        early = picked(rows, near, early_source(c, tile, 24) + 8 * j)
        for strip in range(3):
            late_ref[strip, :, tile * 128 : (tile + 1) * 128] = late[:, strip * 128 : (strip + 1) * 128]
            early_ref[strip, :, tile * 128 : (tile + 1) * 128] = early[:, strip * 128 : (strip + 1) * 128]


def order_query(x):
    shape = jax.ShapeDtypeStruct((3, TOK, 512), jnp.bfloat16)
    return pl.pallas_call(
        order_query_kernel,
        grid=(1,),
        in_specs=[whole(x.shape)],
        out_specs=[whole(shape.shape)] * 2,
        out_shape=[shape, shape],
        compiler_params=pltpu.CompilerParams(vmem_limit_bytes=16 * MIB),
        cost_estimate=pl.CostEstimate(flops=2_500_000_000, bytes_accessed=6_000_000, transcendentals=0),
        name="order_query",
    )(x)


def order_latent_kernel(me_ref, own_ref, own_rope_ref, *refs):
    pieces, (late_ref, early_ref, rope_ref, prev_ref) = refs[:4], refs[4:]
    for offset, piece in zip((0, -1, 1, 2), pieces):
        slot = lax.rem(me_ref[0] + offset % 4, 4)
        prev_ref[pl.ds(pl.multiple_of(slot * 128, 128), 128), :] = piece[...]
    rope_ref[:TOK] = own_rope_ref[...]
    rope_ref[TOK:] = prev_ref[:, 512:]
    c = lax.broadcasted_iota(jnp.int32, (1, 128), 1)
    for part, ref in ((0, own_ref), (1, prev_ref)):
        rows = lambda tile: ref[:, tile * 128 : (tile + 1) * 128]
        for tile in range(4):
            at = slice(tile * 128, (tile + 1) * 128)
            late_ref[part * TOK : (part + 1) * TOK, at] = picked(rows, range(4), late_source(c, tile, 8))
            near = [tile // 2 * 2, tile // 2 * 2 + 1]
            early_ref[part * TOK : (part + 1) * TOK, at] = picked(rows, near, early_source(c, tile, 8))


def order_latent(me, own, own_rope, pieces):
    operands = (own, own_rope, *pieces)
    shapes = [jax.ShapeDtypeStruct((2 * TOK, width), jnp.bfloat16) for width in (512, 512, QK_ROPE)]
    return pl.pallas_call(
        order_latent_kernel,
        grid=(1,),
        in_specs=[SMEM] + [whole(a.shape) for a in operands],
        out_specs=[whole(a.shape) for a in shapes],
        out_shape=shapes,
        scratch_shapes=[pltpu.VMEM((TOK, 512 + QK_ROPE), jnp.bfloat16)],
        compiler_params=pltpu.CompilerParams(vmem_limit_bytes=16 * MIB),
        cost_estimate=pl.CostEstimate(flops=1_000_000_000, bytes_accessed=4_000_000, transcendentals=0),
        name="order_latent",
    )(me.reshape(1), *operands)


def moved(block, axes, distance):
    count = lax.axis_size(axes)
    return lax.ppermute(block, axes, [(i, (i + distance) % count) for i in range(count)])


def local(query_latent, shared_latent, rope_keys, block_order, query_weight, key_weight, value_weight):
    heads = key_weight.shape[1] // QK_NOPE
    me_x = lax.axis_index(X).astype(jnp.int32)
    me_z = lax.axis_index("z").astype(jnp.int32)
    me_core = lax.axis_index("core").astype(jnp.int32)
    cycle = lax.axis_size(("z", "xl"))
    packed_a, packed_b = pack(query_weight, key_weight, value_weight)

    barrier = lax.optimization_barrier
    me_t = lax.axis_index("tensor").astype(jnp.int32)
    quarter = TOK // lax.axis_size("tensor")

    along_x = [packed_a, moved(packed_a, X, 1), moved(packed_a, X, -1), moved(packed_a, X, 2)]
    shard_a = in_order(me_x, (0, -1, 1, 2), along_x)
    shard_a, latent, rope_own, block_order = barrier((shard_a, shared_latent[0], rope_keys[0], block_order))
    gathered_a = lax.all_gather(shard_a, ("z", "core"), axis=0, tiled=True)

    position = lax.axis_index(("z", "xl"))
    order_row = block_order[lax.axis_index(("xh", "core"))]
    seen = (order_row[(position - 1 + cycle) % cycle] < order_row[position]).astype(jnp.int32)
    place = jnp.stack([seen, me_x, me_core])
    mine = jnp.concatenate(
        [lax.dynamic_slice_in_dim(a, me_t * quarter, quarter, 0) for a in (latent, rope_own)], axis=1
    )
    up, down = moved(packed_b, "z", 1), moved(packed_b, "z", -1)
    up2, down2 = moved(packed_b, "z", 2), moved(packed_b, "z", -2)
    up3, down3, up4 = moved(up2, "z", 1), moved(down2, "z", -1), moved(up2, "z", 2)
    own = in_order(me_z, (0, -1, 1, -2, 2, -3, 3, -4), [packed_b, up, down, up2, down2, up3, down3, up4])
    theirs = moved(mine, ("z", "xl"), 1)
    own, theirs, place, rope_own = barrier((own, theirs, place, rope_own))

    before, after = moved(own, X, 1), moved(own, X, -1)
    prev = [theirs, moved(theirs, "tensor", 1), moved(theirs, "tensor", -1), moved(theirs, "tensor", 2)]
    x_a, x_b = order_query(query_latent[0])
    before, after, x_a, x_b = barrier((before, after, x_a, x_b))
    low, high = halves(before, after)
    far_low, far_high = moved(low, X, 1), moved(high, X, -1)
    lat_a, lat_b, rope = order_latent(me_t, latent, rope_own, prev)
    far_low, far_high, lat_a, lat_b, rope = barrier((far_low, far_high, lat_a, lat_b, rope))
    mine = [own, before, after, far_low, far_high]
    pieces = mine + [moved(piece, "core", 1) for piece in mine]

    out, peaks_b = attend(from_ring, GROUPS_B, HEADS_A, "ringed", place, x_b, lat_b, rope, pieces)
    gathered_a = [in_hbm(gathered_a)]
    attended, peaks_a = attend(from_gathered, GROUPS_A, 0, "gathered", place, x_a, lat_a, rope, gathered_a, [out])

    peaks = jnp.concatenate([peaks_a, peaks_b])[:, : GROUPS_A[0], 0].reshape(1, heads)
    everyone = lax.axis_size(GROUP)
    shared = lax.all_to_all(jnp.broadcast_to(peaks[None], (everyone, 1, heads)), GROUP, 0, 0)
    logit_max = jnp.max(shared, axis=(0, 1))
    clip = TAU / jnp.maximum(logit_max, TAU)
    root = jnp.sqrt(clip)
    factors = jnp.concatenate(
        [jnp.broadcast_to(root[:, None], (heads, QK_NOPE)), jnp.broadcast_to(clip[:, None], (heads, QK_ROPE))], axis=1
    ).reshape(1, heads * HEAD)
    clipped_q = (query_weight.astype(jnp.float32) * factors).astype(jnp.bfloat16)
    clipped_k = (key_weight.astype(jnp.float32) * jnp.repeat(root, QK_NOPE)[None]).astype(jnp.bfloat16)
    return (attended[None], logit_max, clipped_q, clipped_k)


def solution(mesh):
    fine = Mesh(mesh.devices.reshape(2, 2, 8, 2, 4), ("xh", "core", "z", "xl", "tensor"))
    dp, ctx = ("xh", "core"), ("z", "xl")
    return jax.shard_map(
        local,
        mesh=fine,
        in_specs=(
            P(dp, ctx, None),
            P(dp, ctx, None),
            P(dp, ctx, None),
            P(),
            P(GROUP, "tensor"),
            P(GROUP, "tensor"),
            P(GROUP, "tensor"),
        ),
        out_specs=(
            P(dp, ctx, "tensor"),
            P("tensor"),
            P(GROUP, "tensor"),
            P(GROUP, "tensor"),
        ),
        check_vma=False,
    )
```

profile of v0, /device:TPU:1, one launch (start us, length us, event | category | flops | bytes accessed | tf_op | source)
XLA Modules:
  0.0 128.4 jit_solution(226871342523748294)
XLA Ops:
  8.3 2.1 %collective-permute-start.7 = (bf16[8,8320]{1,0:T(8,128)(2,1)S(1)}, bf16[8,8320]{1,0:T(8,128)(2,1)S(1)}, u32[]{:S(2)}, u32[]{:S(2)}) collective-permute-start(bf16[8,8320]{1,0:T(8,128)(2,1)S(1)} %get-tuple-element.35.refs_0_), channel_id=1, source_target_pairs={{0,4},{4,128},{128,132},{132,0},{1,5},{5,129},{129,133},{133,1},{2... | collective-permute-start | bytes 399368 | tf_op jit(solution)/shard_map/ppermute | solution.py:337
  10.4 1.4 %collective-permute-start.8 = (bf16[8,8320]{1,0:T(8,128)(2,1)S(1)}, bf16[8,8320]{1,0:T(8,128)(2,1)S(1)}, u32[]{:S(2)}, u32[]{:S(2)}) collective-permute-start(bf16[8,8320]{1,0:T(8,128)(2,1)S(1)} %get-tuple-element.35.refs_0_), channel_id=1, source_target_pairs={{0,132},{4,0},{128,4},{132,128},{1,133},{5,1},{129,5},{133,129},{2... | collective-permute-start | bytes 399368 | tf_op jit(solution)/shard_map/ppermute | solution.py:337
  11.8 1.6 %collective-permute-start.9 = (bf16[8,8320]{1,0:T(8,128)(2,1)S(1)}, bf16[8,8320]{1,0:T(8,128)(2,1)S(1)}, u32[]{:S(2)}, u32[]{:S(2)}) collective-permute-start(bf16[8,8320]{1,0:T(8,128)(2,1)S(1)} %get-tuple-element.35.refs_0_), channel_id=1, source_target_pairs={{0,128},{4,132},{128,0},{132,4},{1,129},{5,133},{129,1},{133,5},{2... | collective-permute-start | bytes 399368 | tf_op jit(solution)/shard_map/ppermute | solution.py:337
  14.4 3.7 %collective-permute-done.9.refs_3_ = bf16[8,8320]{1,0:T(8,128)(2,1)S(1)} collective-permute-done((bf16[8,8320]{1,0:T(8,128)(2,1)S(1)}, bf16[8,8320]{1,0:T(8,128)(2,1)S(1)}, u32[]{:S(2)}, u32[]{:S(2)}) %collective-permute-start.9) | collective-permute-done | bytes 133152 | tf_op jit(solution)/shard_map/ppermute | solution.py:337
  19.0 3.9 %collective-permute-start.2 = (bf16[8,4992]{1,0:T(8,128)(2,1)S(1)}, bf16[8,4992]{1,0:T(8,128)(2,1)S(1)}, u32[]{:S(2)}, u32[]{:S(2)}) collective-permute-start(bf16[8,4992]{1,0:T(8,128)(2,1)S(1)} %get-tuple-element.34.refs_0_), channel_id=1, source_target_pairs={{0,16},{8,24},{16,32},{24,40},{32,48},{40,56},{48,0},{56,8},{1,17}... | collective-permute-start | bytes 239624 | tf_op jit(solution)/shard_map/ppermute | solution.py:337
  22.9 3.1 %collective-permute-start.3 = (bf16[8,4992]{1,0:T(8,128)(2,1)S(1)}, bf16[8,4992]{1,0:T(8,128)(2,1)S(1)}, u32[]{:S(2)}, u32[]{:S(2)}) collective-permute-start(bf16[8,4992]{1,0:T(8,128)(2,1)S(1)} %get-tuple-element.34.refs_0_), channel_id=1, source_target_pairs={{0,48},{8,56},{16,0},{24,8},{32,16},{40,24},{48,32},{56,40},{1,49}... | collective-permute-start | bytes 239624 | tf_op jit(solution)/shard_map/ppermute | solution.py:337
  26.9 2.0 %collective-permute-start.1 = (bf16[8,4992]{1,0:T(8,128)(2,1)S(1)}, bf16[8,4992]{1,0:T(8,128)(2,1)S(1)}, u32[]{:S(2)}, u32[]{:S(2)}) collective-permute-start(bf16[8,4992]{1,0:T(8,128)(2,1)S(1)} %get-tuple-element.34.refs_0_), channel_id=1, source_target_pairs={{0,56},{8,0},{16,8},{24,16},{32,24},{40,32},{48,40},{56,48},{1,57}... | collective-permute-start | bytes 239624 | tf_op jit(solution)/shard_map/ppermute | solution.py:337
  31.7 1.6 %collective-permute-start.6 = (bf16[8,4992]{1,0:T(8,128)(2,1)S(1)}, bf16[8,4992]{1,0:T(8,128)(2,1)S(1)}, u32[]{:S(2)}, u32[]{:S(2)}) collective-permute-start(bf16[8,4992]{1,0:T(8,128)(2,1)S(1)} %collective-permute-done.2.refs_3_), channel_id=1, source_target_pairs={{0,16},{8,24},{16,32},{24,40},{32,48},{40,56},{48,0},{56,8},{1,17}... | collective-permute-start | bytes 239624 | tf_op jit(solution)/shard_map/ppermute | solution.py:337
  34.3 3.2 %collective-permute-done.6.refs_7_ = bf16[8,4992]{1,0:T(8,128)(2,1)S(1)} collective-permute-done((bf16[8,4992]{1,0:T(8,128)(2,1)S(1)}, bf16[8,4992]{1,0:T(8,128)(2,1)S(1)}, u32[]{:S(2)}, u32[]{:S(2)}) %collective-permute-start.6) | collective-permute-done | bytes 79904 | tf_op jit(solution)/shard_map/ppermute | solution.py:337
  37.5 2.0 %collective-permute-done.5.refs_6_ = bf16[8,4992]{1,0:T(8,128)(2,1)S(1)} collective-permute-done((bf16[8,4992]{1,0:T(8,128)(2,1)S(1)}, bf16[8,4992]{1,0:T(8,128)(2,1)S(1)}, u32[]{:S(2)}, u32[]{:S(2)}) %collective-permute-start.5) | collective-permute-done | bytes 79904 | tf_op jit(solution)/shard_map/ppermute | solution.py:337
  39.6 2.1 %collective-permute-start.11 = (bf16[64,4992]{1,0:T(8,128)(2,1)S(1)}, bf16[64,4992]{1,0:T(8,128)(2,1)S(1)}, u32[]{:S(2)}, u32[]{:S(2)}) collective-permute-start(bf16[64,4992]{1,0:T(8,128)(2,1)S(1)} %bitcast.13), channel_id=1, source_target_pairs={{0,4},{4,128},{128,132},{132,0},{1,5},{5,129},{129,133},{133,1},{2... | collective-permute-start | bytes 1916936 | tf_op jit(solution)/shard_map/ppermute | solution.py:337
  42.3 1.3 %collective-permute-start.15 = (bf16[128,576]{1,0:T(8,128)(2,1)S(1)}, bf16[128,576]{1,0:T(8,128)(2,1)S(1)}, u32[]{:S(2)}, u32[]{:S(2)}) collective-permute-start(bf16[128,576]{1,0:T(8,128)(2,1)S(1)} %collective-permute-done.10.refs_0_), channel_id=1, source_target_pairs={{0,1},{1,2},{2,3},{3,0},{4,5},{5,6},{6,7},{7,4},{8,9},{9,10},{10,1... | collective-permute-start | bytes 442376 | tf_op jit(solution)/shard_map/ppermute | solution.py:337
  43.6 1.5 %collective-permute-start.16 = (bf16[128,576]{1,0:T(8,128)(2,1)S(1)}, bf16[128,576]{1,0:T(8,128)(2,1)S(1)}, u32[]{:S(2)}, u32[]{:S(2)}) collective-permute-start(bf16[128,576]{1,0:T(8,128)(2,1)S(1)} %collective-permute-done.10.refs_0_), channel_id=1, source_target_pairs={{0,3},{1,0},{2,1},{3,2},{4,7},{5,4},{6,5},{7,6},{8,11},{9,8},{10,9... | collective-permute-start | bytes 442376 | tf_op jit(solution)/shard_map/ppermute | solution.py:337
  45.1 1.6 %collective-permute-start.17 = (bf16[128,576]{1,0:T(8,128)(2,1)S(1)}, bf16[128,576]{1,0:T(8,128)(2,1)S(1)}, u32[]{:S(2)}, u32[]{:S(2)}) collective-permute-start(bf16[128,576]{1,0:T(8,128)(2,1)S(1)} %collective-permute-done.10.refs_0_), channel_id=1, source_target_pairs={{0,2},{1,3},{2,0},{3,1},{4,6},{5,7},{6,4},{7,5},{8,10},{9,11},{10,... | collective-permute-start | bytes 442376 | tf_op jit(solution)/shard_map/ppermute | solution.py:337
  46.7 3.5 %order_query.1 = (bf16[3,512,512]{2,1,0:T(8,128)(2,1)S(1)}, bf16[3,512,512]{2,1,0:T(8,128)(2,1)S(1)}) custom-call(bf16[512,1536]{1,0:T(8,128)(2,1)S(1)} %bitcast.21), custom_call_target="tpu_custom_call" | custom-call | flops 2500000000 | bytes 6000000 | tf_op jit(solution)/shard_map/order_query/pallas_call | solution.py:290
  52.1 1.3 %collective-permute-done.12.after_ref.rest_2_ = bf16[64,4992]{1,0:T(8,128)(2,1)S(1)} collective-permute-done((bf16[64,4992]{1,0:T(8,128)(2,1)S(1)}, bf16[64,4992]{1,0:T(8,128)(2,1)S(1)}, u32[]{:S(2)}, u32[]{:S(2)}) %collective-permute-start.12) | collective-permute-done | bytes 639008 | tf_op jit(solution)/shard_map/ppermute | solution.py:337
  53.8 2.4 %collective-permute-start.14 = (bf16[32,4992]{1,0:T(8,128)(2,1)S(1)}, bf16[32,4992]{1,0:T(8,128)(2,1)S(1)}, u32[]{:S(2)}, u32[]{:S(2)}) collective-permute-start(bf16[32,4992]{1,0:T(8,128)(2,1)S(1)} %get-tuple-element.47), channel_id=1, source_target_pairs={{0,132},{4,0},{128,4},{132,128},{1,133},{5,1},{129,5},{133,129},{2... | collective-permute-start | bytes 958472 | tf_op jit(solution)/shard_map/ppermute | solution.py:337
  56.2 7.0 %collective-permute-start.18 = (bf16[64,4992]{1,0:T(8,128)(2,1)S(1)}, bf16[64,4992]{1,0:T(8,128)(2,1)S(1)}, u32[]{:S(2)}, u32[]{:S(2)}) collective-permute-start(bf16[64,4992]{1,0:T(8,128)(2,1)S(1)} %bitcast.15), channel_id=1, source_target_pairs={{0,64},{64,0},{1,65},{65,1},{2,66},{66,2},{3,67},{67,3},{4,68},{68... | collective-permute-start | bytes 1916936 | tf_op jit(solution)/shard_map/ppermute | solution.py:337
  63.8 1.9 %order_latent.1 = (bf16[1024,512]{1,0:T(8,128)(2,1)S(1)}, bf16[1024,512]{1,0:T(8,128)(2,1)S(1)}, bf16[1024,64]{1,0:T(8,128)(2,1)S(1)}) custom-call(s32[1]{0:T(128)} %bitcast.9.me_ref, bf16[512,512]{1,0:T(8,128)(2,1)S(1)} %bitcast.20, bf16[512,64]{1,0:T(8,128)(2,1)S(1)} %bitcast.18, bf16[128,576]{1,0:T(8,128)(2,1)S(1)} %collective-permute-done.10.refs_0_, ...), custom_call_target="tpu_custom_call" | custom-call | flops 1000000000 | bytes 4000000 | tf_op jit(solution)/shard_map/order_latent/pallas_call | solution.py:322
  66.7 1.5 %collective-permute-start.21 = (bf16[32,4992]{1,0:T(8,128)(2,1)S(1)}, bf16[32,4992]{1,0:T(8,128)(2,1)S(1)}, u32[]{:S(2)}, u32[]{:S(2)}) collective-permute-start(bf16[32,4992]{1,0:T(8,128)(2,1)S(1)} %collective-permute-done.13.rest_3_), channel_id=1, source_target_pairs={{0,64},{64,0},{1,65},{65,1},{2,66},{66,2},{3,67},{67,3},{4,68},{68... | collective-permute-start | bytes 958472 | tf_op jit(solution)/shard_map/ppermute | solution.py:337
  68.2 1.2 collective-permute-done.21.rest_8_
  69.9 11.8 %ringed.1 = (bf16[512,2048]{1,0:T(8,128)(2,1)}, f32[3,8,128]{2,1,0:T(8,128)S(1)}) custom-call(s32[3]{0:T(128)S(1)} %pad_add_fusion.place_ref, bf16[3,512,512]{2,1,0:T(8,128)(2,1)S(1)} %get-tuple-element.56.x_ref, bf16[1024,512]{1,0:T(8,128)(2,1)S(1)} %get-tuple-element.57.lat_ref, bf16[1024,64]{1,0:T(8,128)(2,1)S(1)} %get-tuple-element.54.rope_ref, ...), custom_call_target="tpu_custom_call" | custom-call | flops 5400000000 | bytes 6000000 | tf_op jit(solution)/shard_map/ringed/pallas_call | solution.py:158
  81.8 18.9 %gathered.1 = (bf16[512,2048]{1,0:T(8,128)(2,1)}, f32[5,8,128]{2,1,0:T(8,128)S(1)}) custom-call(s32[3]{0:T(128)S(1)} %pad_add_fusion.place_ref, bf16[3,512,512]{2,1,0:T(8,128)(2,1)} %copy-done.4, bf16[1024,512]{1,0:T(8,128)(2,1)} %copy-done.2, bf16[1024,64]{1,0:T(8,128)(2,1)} %copy-done.3, ...), custom_call_target="tpu_custom_call", output_to_operand_aliasing={{0}: (5, {})} | custom-call | flops 8999999488 | bytes 10000000 | tf_op jit(solution)/shard_map/gathered/pallas_call | solution.py:158
  100.9 18.9 %all_to_all.5 = f32[64,1,16]{2,1,0:T(1,128)S(1)} all-to-all(f32[64,1,16]{2,1,0:T(1,128)S(1)} %broadcast_in_dim.12), channel_id=1, replica_groups=mesh['xh'=2,'core'=2,'z'=8,'xl'=2,'tensor'=4] {'xh','core','z','xl'}, dimensions={0} | all-to-all | bytes 8192 | tf_op jit(solution)/shard_map/all_to_all | solution.py:388
  (70 shorter events, 13.2 us)
Async XLA Ops:
  7.2 74.5 %all-gather.2.cloned.1.call-start = ((), (), s32[]{:S(2)}) async-start(), calls=%async_computation.1 | async-start | bytes 9052160 | tf_op jit(solution)/shard_map/all_gather | solution.py:355
  8.3 6.1 %collective-permute-start.7 = (bf16[8,8320]{1,0:T(8,128)(2,1)S(1)}, bf16[8,8320]{1,0:T(8,128)(2,1)S(1)}, u32[]{:S(2)}, u32[]{:S(2)}) collective-permute-start(bf16[8,8320]{1,0:T(8,128)(2,1)S(1)} %get-tuple-element.35.refs_0_), channel_id=1, source_target_pairs={{0,4},{4,128},{128,132},{132,0},{1,5},{5,129},{129,133},{133,1},{2... | collective-permute-start | bytes 399368 | tf_op jit(solution)/shard_map/ppermute | solution.py:337
  10.4 4.0 %collective-permute-start.8 = (bf16[8,8320]{1,0:T(8,128)(2,1)S(1)}, bf16[8,8320]{1,0:T(8,128)(2,1)S(1)}, u32[]{:S(2)}, u32[]{:S(2)}) collective-permute-start(bf16[8,8320]{1,0:T(8,128)(2,1)S(1)} %get-tuple-element.35.refs_0_), channel_id=1, source_target_pairs={{0,132},{4,0},{128,4},{132,128},{1,133},{5,1},{129,5},{133,129},{2... | collective-permute-start | bytes 399368 | tf_op jit(solution)/shard_map/ppermute | solution.py:337
  11.8 6.4 %collective-permute-start.9 = (bf16[8,8320]{1,0:T(8,128)(2,1)S(1)}, bf16[8,8320]{1,0:T(8,128)(2,1)S(1)}, u32[]{:S(2)}, u32[]{:S(2)}) collective-permute-start(bf16[8,8320]{1,0:T(8,128)(2,1)S(1)} %get-tuple-element.35.refs_0_), channel_id=1, source_target_pairs={{0,128},{4,132},{128,0},{132,4},{1,129},{5,133},{129,1},{133,5},{2... | collective-permute-start | bytes 399368 | tf_op jit(solution)/shard_map/ppermute | solution.py:337
  19.0 9.9 %collective-permute-start.2 = (bf16[8,4992]{1,0:T(8,128)(2,1)S(1)}, bf16[8,4992]{1,0:T(8,128)(2,1)S(1)}, u32[]{:S(2)}, u32[]{:S(2)}) collective-permute-start(bf16[8,4992]{1,0:T(8,128)(2,1)S(1)} %get-tuple-element.34.refs_0_), channel_id=1, source_target_pairs={{0,16},{8,24},{16,32},{24,40},{32,48},{40,56},{48,0},{56,8},{1,17}... | collective-permute-start | bytes 239624 | tf_op jit(solution)/shard_map/ppermute | solution.py:337
  22.9 8.8 %collective-permute-start.3 = (bf16[8,4992]{1,0:T(8,128)(2,1)S(1)}, bf16[8,4992]{1,0:T(8,128)(2,1)S(1)}, u32[]{:S(2)}, u32[]{:S(2)}) collective-permute-start(bf16[8,4992]{1,0:T(8,128)(2,1)S(1)} %get-tuple-element.34.refs_0_), channel_id=1, source_target_pairs={{0,48},{8,56},{16,0},{24,8},{32,16},{40,24},{48,32},{56,40},{1,49}... | collective-permute-start | bytes 239624 | tf_op jit(solution)/shard_map/ppermute | solution.py:337
  26.0 7.3 %collective-permute-start = (bf16[8,4992]{1,0:T(8,128)(2,1)S(1)}, bf16[8,4992]{1,0:T(8,128)(2,1)S(1)}, u32[]{:S(2)}, u32[]{:S(2)}) collective-permute-start(bf16[8,4992]{1,0:T(8,128)(2,1)S(1)} %get-tuple-element.34.refs_0_), channel_id=1, source_target_pairs={{0,8},{8,16},{16,24},{24,32},{32,40},{40,48},{48,56},{56,0},{1,9},... | collective-permute-start | bytes 239624 | tf_op jit(solution)/shard_map/ppermute | solution.py:337
  26.8 12.7 %collective-permute-start.10 = (bf16[128,576]{1,0:T(8,128)(2,1)S(1)}, bf16[128,576]{1,0:T(8,128)(2,1)S(1)}, u32[]{:S(2)}, u32[]{:S(2)}) collective-permute-start(bf16[128,576]{1,0:T(8,128)(2,1)S(1)} %pad_maximum_fusion), channel_id=1, source_target_pairs={{0,4},{4,8},{8,12},{12,16},{16,20},{20,24},{24,28},{28,32},{32,36}... | collective-permute-start | bytes 442376 | tf_op jit(solution)/shard_map/ppermute | solution.py:337
  26.9 7.4 %collective-permute-start.1 = (bf16[8,4992]{1,0:T(8,128)(2,1)S(1)}, bf16[8,4992]{1,0:T(8,128)(2,1)S(1)}, u32[]{:S(2)}, u32[]{:S(2)}) collective-permute-start(bf16[8,4992]{1,0:T(8,128)(2,1)S(1)} %get-tuple-element.34.refs_0_), channel_id=1, source_target_pairs={{0,56},{8,0},{16,8},{24,16},{32,24},{40,32},{48,40},{56,48},{1,57}... | collective-permute-start | bytes 239624 | tf_op jit(solution)/shard_map/ppermute | solution.py:337
  28.9 5.4 %collective-permute-start.4 = (bf16[8,4992]{1,0:T(8,128)(2,1)S(1)}, bf16[8,4992]{1,0:T(8,128)(2,1)S(1)}, u32[]{:S(2)}, u32[]{:S(2)}) collective-permute-start(bf16[8,4992]{1,0:T(8,128)(2,1)S(1)} %collective-permute-done.2.refs_3_), channel_id=1, source_target_pairs={{0,8},{8,16},{16,24},{24,32},{32,40},{40,48},{48,56},{56,0},{1,9},... | collective-permute-start | bytes 239624 | tf_op jit(solution)/shard_map/ppermute | solution.py:337
  31.7 5.8 %collective-permute-start.6 = (bf16[8,4992]{1,0:T(8,128)(2,1)S(1)}, bf16[8,4992]{1,0:T(8,128)(2,1)S(1)}, u32[]{:S(2)}, u32[]{:S(2)}) collective-permute-start(bf16[8,4992]{1,0:T(8,128)(2,1)S(1)} %collective-permute-done.2.refs_3_), channel_id=1, source_target_pairs={{0,16},{8,24},{16,32},{24,40},{32,48},{40,56},{48,0},{56,8},{1,17}... | collective-permute-start | bytes 239624 | tf_op jit(solution)/shard_map/ppermute | solution.py:337
  33.3 6.1 %collective-permute-start.5 = (bf16[8,4992]{1,0:T(8,128)(2,1)S(1)}, bf16[8,4992]{1,0:T(8,128)(2,1)S(1)}, u32[]{:S(2)}, u32[]{:S(2)}) collective-permute-start(bf16[8,4992]{1,0:T(8,128)(2,1)S(1)} %collective-permute-done.3.refs_4_), channel_id=1, source_target_pairs={{0,56},{8,0},{16,8},{24,16},{32,24},{40,32},{48,40},{56,48},{1,57}... | collective-permute-start | bytes 239624 | tf_op jit(solution)/shard_map/ppermute | solution.py:337
  39.6 12.5 %collective-permute-start.11 = (bf16[64,4992]{1,0:T(8,128)(2,1)S(1)}, bf16[64,4992]{1,0:T(8,128)(2,1)S(1)}, u32[]{:S(2)}, u32[]{:S(2)}) collective-permute-start(bf16[64,4992]{1,0:T(8,128)(2,1)S(1)} %bitcast.13), channel_id=1, source_target_pairs={{0,4},{4,128},{128,132},{132,0},{1,5},{5,129},{129,133},{133,1},{2... | collective-permute-start | bytes 1916936 | tf_op jit(solution)/shard_map/ppermute | solution.py:337
  41.6 11.8 %collective-permute-start.12 = (bf16[64,4992]{1,0:T(8,128)(2,1)S(1)}, bf16[64,4992]{1,0:T(8,128)(2,1)S(1)}, u32[]{:S(2)}, u32[]{:S(2)}) collective-permute-start(bf16[64,4992]{1,0:T(8,128)(2,1)S(1)} %bitcast.14), channel_id=1, source_target_pairs={{0,132},{4,0},{128,4},{132,128},{1,133},{5,1},{129,5},{133,129},{2... | collective-permute-start | bytes 1916936 | tf_op jit(solution)/shard_map/ppermute | solution.py:337
  42.3 13.9 %collective-permute-start.15 = (bf16[128,576]{1,0:T(8,128)(2,1)S(1)}, bf16[128,576]{1,0:T(8,128)(2,1)S(1)}, u32[]{:S(2)}, u32[]{:S(2)}) collective-permute-start(bf16[128,576]{1,0:T(8,128)(2,1)S(1)} %collective-permute-done.10.refs_0_), channel_id=1, source_target_pairs={{0,1},{1,2},{2,3},{3,0},{4,5},{5,6},{6,7},{7,4},{8,9},{9,10},{10,1... | collective-permute-start | bytes 442376 | tf_op jit(solution)/shard_map/ppermute | solution.py:337
  43.6 19.6 %collective-permute-start.16 = (bf16[128,576]{1,0:T(8,128)(2,1)S(1)}, bf16[128,576]{1,0:T(8,128)(2,1)S(1)}, u32[]{:S(2)}, u32[]{:S(2)}) collective-permute-start(bf16[128,576]{1,0:T(8,128)(2,1)S(1)} %collective-permute-done.10.refs_0_), channel_id=1, source_target_pairs={{0,3},{1,0},{2,1},{3,2},{4,7},{5,4},{6,5},{7,6},{8,11},{9,8},{10,9... | collective-permute-start | bytes 442376 | tf_op jit(solution)/shard_map/ppermute | solution.py:337
  45.1 18.2 %collective-permute-start.17 = (bf16[128,576]{1,0:T(8,128)(2,1)S(1)}, bf16[128,576]{1,0:T(8,128)(2,1)S(1)}, u32[]{:S(2)}, u32[]{:S(2)}) collective-permute-start(bf16[128,576]{1,0:T(8,128)(2,1)S(1)} %collective-permute-done.10.refs_0_), channel_id=1, source_target_pairs={{0,2},{1,3},{2,0},{3,1},{4,6},{5,7},{6,4},{7,5},{8,10},{9,11},{10,... | collective-permute-start | bytes 442376 | tf_op jit(solution)/shard_map/ppermute | solution.py:337
  53.4 13.2 %collective-permute-start.13 = (bf16[32,4992]{1,0:T(8,128)(2,1)S(1)}, bf16[32,4992]{1,0:T(8,128)(2,1)S(1)}, u32[]{:S(2)}, u32[]{:S(2)}) collective-permute-start(bf16[32,4992]{1,0:T(8,128)(2,1)S(1)} %get-tuple-element.46), channel_id=1, source_target_pairs={{0,4},{4,128},{128,132},{132,0},{1,5},{5,129},{129,133},{133,1},{2... | collective-permute-start | bytes 958472 | tf_op jit(solution)/shard_map/ppermute | solution.py:337
  53.8 12.9 %collective-permute-start.14 = (bf16[32,4992]{1,0:T(8,128)(2,1)S(1)}, bf16[32,4992]{1,0:T(8,128)(2,1)S(1)}, u32[]{:S(2)}, u32[]{:S(2)}) collective-permute-start(bf16[32,4992]{1,0:T(8,128)(2,1)S(1)} %get-tuple-element.47), channel_id=1, source_target_pairs={{0,132},{4,0},{128,4},{132,128},{1,133},{5,1},{129,5},{133,129},{2... | collective-permute-start | bytes 958472 | tf_op jit(solution)/shard_map/ppermute | solution.py:337
  56.2 12.0 %collective-permute-start.18 = (bf16[64,4992]{1,0:T(8,128)(2,1)S(1)}, bf16[64,4992]{1,0:T(8,128)(2,1)S(1)}, u32[]{:S(2)}, u32[]{:S(2)}) collective-permute-start(bf16[64,4992]{1,0:T(8,128)(2,1)S(1)} %bitcast.15), channel_id=1, source_target_pairs={{0,64},{64,0},{1,65},{65,1},{2,66},{66,2},{3,67},{67,3},{4,68},{68... | collective-permute-start | bytes 1916936 | tf_op jit(solution)/shard_map/ppermute | solution.py:337
  63.3 6.7 %collective-permute-start.19 = (bf16[64,4992]{1,0:T(8,128)(2,1)S(1)}, bf16[64,4992]{1,0:T(8,128)(2,1)S(1)}, u32[]{:S(2)}, u32[]{:S(2)}) collective-permute-start(bf16[64,4992]{1,0:T(8,128)(2,1)S(1)} %collective-permute-done.11.before_ref.rest_1_), channel_id=1, source_target_pairs={{0,64},{64,0},{1,65},{65,1},{2,66},{66,2},{3,67},{67,3},{4,68},{68... | collective-permute-start | bytes 1916936 | tf_op jit(solution)/shard_map/ppermute | solution.py:337
  63.3 6.6 %collective-permute-start.20 = (bf16[64,4992]{1,0:T(8,128)(2,1)S(1)}, bf16[64,4992]{1,0:T(8,128)(2,1)S(1)}, u32[]{:S(2)}, u32[]{:S(2)}) collective-permute-start(bf16[64,4992]{1,0:T(8,128)(2,1)S(1)} %collective-permute-done.12.after_ref.rest_2_), channel_id=1, source_target_pairs={{0,64},{64,0},{1,65},{65,1},{2,66},{66,2},{3,67},{67,3},{4,68},{68... | collective-permute-start | bytes 1916936 | tf_op jit(solution)/shard_map/ppermute | solution.py:337
  66.7 2.8 %collective-permute-start.21 = (bf16[32,4992]{1,0:T(8,128)(2,1)S(1)}, bf16[32,4992]{1,0:T(8,128)(2,1)S(1)}, u32[]{:S(2)}, u32[]{:S(2)}) collective-permute-start(bf16[32,4992]{1,0:T(8,128)(2,1)S(1)} %collective-permute-done.13.rest_3_), channel_id=1, source_target_pairs={{0,64},{64,0},{1,65},{65,1},{2,66},{66,2},{3,67},{67,3},{4,68},{68... | collective-permute-start | bytes 958472 | tf_op jit(solution)/shard_map/ppermute | solution.py:337
  68.2 1.7 %collective-permute-start.22 = (bf16[32,4992]{1,0:T(8,128)(2,1)S(1)}, bf16[32,4992]{1,0:T(8,128)(2,1)S(1)}, u32[]{:S(2)}, u32[]{:S(2)}) collective-permute-start(bf16[32,4992]{1,0:T(8,128)(2,1)S(1)} %collective-permute-done.14.rest_4_), channel_id=1, source_target_pairs={{0,64},{64,0},{1,65},{65,1},{2,66},{66,2},{3,67},{67,3},{4,68},{68... | collective-permute-start | bytes 958472 | tf_op jit(solution)/shard_map/ppermute | solution.py:337
  (9 other events, 178.2 us)
Sparse Core Ops, SparseCore 0:
  19.2 62.4 all-gather.1
where the time goes:
time: 129 us; the launch traced here: 128 us
  Pallas kernels  38.1 us (30%)
  starting transfers between devices  37.3 us (29%)
  blocking collectives  18.9 us (15%)
  between operations  15.5 us (12%)
  waiting for transfers between devices  12.8 us (10%)
  local copies, waits for them, and re-layouts  4.12 us (3%)
  other arithmetic  1.6 us (1%)
    ppermute x23, starting transfers between devices, moved(): lax.ppermute(block, axes, [(i, (i + distance) % count) for i in range(cou...  37.3 us
    pallas_call x2, Pallas kernels, attend(): pl.pallas_call(functools.partial(attend_kernel, rows_of, heads, steps, co...  30.7 us
    all_to_all x1, blocking collectives, local(): lax.all_to_all(jnp.broadcast_to(peaks[None], (everyone, 1, heads)), GROUP...  18.9 us
    ppermute x23, waiting for transfers between devices, moved(): lax.ppermute(block, axes, [(i, (i + distance) % count) for i in range(cou...  12.7 us
    pallas_call x1, Pallas kernels, order_query(): pl.pallas_call(order_query_kernel, grid=(1,), in_specs=[whole(x.shape)],...  3.45 us
    unnamed x19, local copies, waits for them, and re-layouts  3.12 us
  transfers between devices with their start and end apart: 24, of which 7 were waited for; matrix products, arithmetic and copies ran while one was open for 1% of the time, Pallas kernels for 13%

commit v1 on v0

--- a/solution.py
+++ b/solution.py
@@ -363,8 +363,9 @@
     )
     up, down = moved(packed_b, "z", 1), moved(packed_b, "z", -1)
     up2, down2 = moved(packed_b, "z", 2), moved(packed_b, "z", -2)
-    up3, down3, up4 = moved(up2, "z", 1), moved(down2, "z", -1), moved(up2, "z", 2)
-    own = in_order(me_z, (0, -1, 1, -2, 2, -3, 3, -4), [packed_b, up, down, up2, down2, up3, down3, up4])
+    up3, down3 = moved(up2, "z", 1), moved(down2, "z", -1)
+    down4 = moved(down3, "z", -1)
+    own = in_order(me_z, (0, -1, 1, -2, 2, -3, 3, 4), [packed_b, up, down, up2, down2, up3, down3, down4])
     theirs = moved(mine, ("z", "xl"), 1)
     own, theirs, place, rope_own = barrier((own, theirs, place, rope_own))
 

time: 129 us -> 129 us (level)
  starting transfers between devices: 37.3 us -> 42.8 us
  blocking collectives: 18.9 us -> 14.9 us
    ppermute x23, starting transfers between devices: 37.3 us -> 42.7 us  [moved(): lax.ppermute(block, axes, [(i, (i + distance) % count) for i in range(cou...]
    all_to_all x1, blocking collectives: 18.9 us -> 14.9 us  [local(): lax.all_to_all(jnp.broadcast_to(peaks[None], (everyone, 1, heads)), GROUP...]
where the time goes in v1:
time: 129 us
  starting transfers between devices  42.8 us (33%)
  Pallas kernels  38.1 us (30%)
  between operations  15.6 us (12%)
  blocking collectives  14.9 us (12%)
  waiting for transfers between devices  12 us (9%)
  local copies, waits for them, and re-layouts  4.13 us (3%)
  other arithmetic  1.6 us (1%)
    ppermute x23, starting transfers between devices, moved(): lax.ppermute(block, axes, [(i, (i + distance) % count) for i in range(cou...  42.7 us
    pallas_call x2, Pallas kernels, attend(): pl.pallas_call(functools.partial(attend_kernel, rows_of, heads, steps, co...  30.7 us
    all_to_all x1, blocking collectives, local(): lax.all_to_all(jnp.broadcast_to(peaks[None], (everyone, 1, heads)), GROUP...  14.9 us
    ppermute x23, waiting for transfers between devices, moved(): lax.ppermute(block, axes, [(i, (i + distance) % count) for i in range(cou...  12 us
    pallas_call x1, Pallas kernels, order_query(): pl.pallas_call(order_query_kernel, grid=(1,), in_specs=[whole(x.shape)],...  3.45 us
    unnamed x19, local copies, waits for them, and re-layouts  3.12 us
  transfers between devices with their start and end apart: 24, of which 7 were waited for; matrix products, arithmetic and copies ran while one was open for 1% of the time, Pallas kernels for 13%

profile of v1, /device:TPU:1, one launch (start us, length us, event | category | flops | bytes accessed | tf_op | source)
XLA Modules:
  0.0 129.1 jit_solution(5166597800634598716)
XLA Ops:
  8.3 2.1 %collective-permute-start.7 = (bf16[8,8320]{1,0:T(8,128)(2,1)S(1)}, bf16[8,8320]{1,0:T(8,128)(2,1)S(1)}, u32[]{:S(2)}, u32[]{:S(2)}) collective-permute-start(bf16[8,8320]{1,0:T(8,128)(2,1)S(1)} %get-tuple-element.35.refs_0_), channel_id=1, source_target_pairs={{0,4},{4,128},{128,132},{132,0},{1,5},{5,129},{129,133},{133,1},{2... | collective-permute-start | bytes 399368 | tf_op jit(solution)/shard_map/ppermute | solution.py:337
  10.4 1.4 %collective-permute-start.8 = (bf16[8,8320]{1,0:T(8,128)(2,1)S(1)}, bf16[8,8320]{1,0:T(8,128)(2,1)S(1)}, u32[]{:S(2)}, u32[]{:S(2)}) collective-permute-start(bf16[8,8320]{1,0:T(8,128)(2,1)S(1)} %get-tuple-element.35.refs_0_), channel_id=1, source_target_pairs={{0,132},{4,0},{128,4},{132,128},{1,133},{5,1},{129,5},{133,129},{2... | collective-permute-start | bytes 399368 | tf_op jit(solution)/shard_map/ppermute | solution.py:337
  11.8 1.6 %collective-permute-start.9 = (bf16[8,8320]{1,0:T(8,128)(2,1)S(1)}, bf16[8,8320]{1,0:T(8,128)(2,1)S(1)}, u32[]{:S(2)}, u32[]{:S(2)}) collective-permute-start(bf16[8,8320]{1,0:T(8,128)(2,1)S(1)} %get-tuple-element.35.refs_0_), channel_id=1, source_target_pairs={{0,128},{4,132},{128,0},{132,4},{1,129},{5,133},{129,1},{133,5},{2... | collective-permute-start | bytes 399368 | tf_op jit(solution)/shard_map/ppermute | solution.py:337
  14.4 3.7 %collective-permute-done.9.refs_3_ = bf16[8,8320]{1,0:T(8,128)(2,1)S(1)} collective-permute-done((bf16[8,8320]{1,0:T(8,128)(2,1)S(1)}, bf16[8,8320]{1,0:T(8,128)(2,1)S(1)}, u32[]{:S(2)}, u32[]{:S(2)}) %collective-permute-start.9) | collective-permute-done | bytes 133152 | tf_op jit(solution)/shard_map/ppermute | solution.py:337
  19.0 6.9 %collective-permute-start.3 = (bf16[8,4992]{1,0:T(8,128)(2,1)S(1)}, bf16[8,4992]{1,0:T(8,128)(2,1)S(1)}, u32[]{:S(2)}, u32[]{:S(2)}) collective-permute-start(bf16[8,4992]{1,0:T(8,128)(2,1)S(1)} %get-tuple-element.34.refs_0_), channel_id=1, source_target_pairs={{0,48},{8,56},{16,0},{24,8},{32,16},{40,24},{48,32},{56,40},{1,49}... | collective-permute-start | bytes 239624 | tf_op jit(solution)/shard_map/ppermute | solution.py:337
  25.9 2.2 %collective-permute-done.3.refs_4_ = bf16[8,4992]{1,0:T(8,128)(2,1)S(1)} collective-permute-done((bf16[8,4992]{1,0:T(8,128)(2,1)S(1)}, bf16[8,4992]{1,0:T(8,128)(2,1)S(1)}, u32[]{:S(2)}, u32[]{:S(2)}) %collective-permute-start.3) | collective-permute-done | bytes 79904 | tf_op jit(solution)/shard_map/ppermute | solution.py:337
  28.1 2.9 %collective-permute-start.5 = (bf16[8,4992]{1,0:T(8,128)(2,1)S(1)}, bf16[8,4992]{1,0:T(8,128)(2,1)S(1)}, u32[]{:S(2)}, u32[]{:S(2)}) collective-permute-start(bf16[8,4992]{1,0:T(8,128)(2,1)S(1)} %collective-permute-done.3.refs_4_), channel_id=1, source_target_pairs={{0,56},{8,0},{16,8},{24,16},{32,24},{40,32},{48,40},{56,48},{1,57}... | collective-permute-start | bytes 239624 | tf_op jit(solution)/shard_map/ppermute | solution.py:337
  31.3 2.7 %collective-permute-start.1 = (bf16[8,4992]{1,0:T(8,128)(2,1)S(1)}, bf16[8,4992]{1,0:T(8,128)(2,1)S(1)}, u32[]{:S(2)}, u32[]{:S(2)}) collective-permute-start(bf16[8,4992]{1,0:T(8,128)(2,1)S(1)} %get-tuple-element.34.refs_0_), channel_id=1, source_target_pairs={{0,56},{8,0},{16,8},{24,16},{32,24},{40,32},{48,40},{56,48},{1,57}... | collective-permute-start | bytes 239624 | tf_op jit(solution)/shard_map/ppermute | solution.py:337
  35.8 2.7 %collective-permute-start.6 = (bf16[8,4992]{1,0:T(8,128)(2,1)S(1)}, bf16[8,4992]{1,0:T(8,128)(2,1)S(1)}, u32[]{:S(2)}, u32[]{:S(2)}) collective-permute-start(bf16[8,4992]{1,0:T(8,128)(2,1)S(1)} %collective-permute-done.5.refs_6_), channel_id=1, source_target_pairs={{0,56},{8,0},{16,8},{24,16},{32,24},{40,32},{48,40},{56,48},{1,57}... | collective-permute-start | bytes 239624 | tf_op jit(solution)/shard_map/ppermute | solution.py:337
  38.7 1.8 %collective-permute-done.4.refs_5_ = bf16[8,4992]{1,0:T(8,128)(2,1)S(1)} collective-permute-done((bf16[8,4992]{1,0:T(8,128)(2,1)S(1)}, bf16[8,4992]{1,0:T(8,128)(2,1)S(1)}, u32[]{:S(2)}, u32[]{:S(2)}) %collective-permute-start.4) | collective-permute-done | bytes 79904 | tf_op jit(solution)/shard_map/ppermute | solution.py:337
  40.5 1.9 %collective-permute-done.6.refs_7_ = bf16[8,4992]{1,0:T(8,128)(2,1)S(1)} collective-permute-done((bf16[8,4992]{1,0:T(8,128)(2,1)S(1)}, bf16[8,4992]{1,0:T(8,128)(2,1)S(1)}, u32[]{:S(2)}, u32[]{:S(2)}) %collective-permute-start.6) | collective-permute-done | bytes 79904 | tf_op jit(solution)/shard_map/ppermute | solution.py:337
  43.4 1.9 %collective-permute-start.12 = (bf16[64,4992]{1,0:T(8,128)(2,1)S(1)}, bf16[64,4992]{1,0:T(8,128)(2,1)S(1)}, u32[]{:S(2)}, u32[]{:S(2)}) collective-permute-start(bf16[64,4992]{1,0:T(8,128)(2,1)S(1)} %bitcast.14), channel_id=1, source_target_pairs={{0,132},{4,0},{128,4},{132,128},{1,133},{5,1},{129,5},{133,129},{2... | collective-permute-start | bytes 1916936 | tf_op jit(solution)/shard_map/ppermute | solution.py:337
  45.3 1.2 collective-permute-start.15
  46.5 1.4 %collective-permute-start.16 = (bf16[128,576]{1,0:T(8,128)(2,1)S(1)}, bf16[128,576]{1,0:T(8,128)(2,1)S(1)}, u32[]{:S(2)}, u32[]{:S(2)}) collective-permute-start(bf16[128,576]{1,0:T(8,128)(2,1)S(1)} %collective-permute-done.10.refs_0_), channel_id=1, source_target_pairs={{0,3},{1,0},{2,1},{3,2},{4,7},{5,4},{6,5},{7,6},{8,11},{9,8},{10,9... | collective-permute-start | bytes 442376 | tf_op jit(solution)/shard_map/ppermute | solution.py:337
  47.9 1.6 %collective-permute-start.17 = (bf16[128,576]{1,0:T(8,128)(2,1)S(1)}, bf16[128,576]{1,0:T(8,128)(2,1)S(1)}, u32[]{:S(2)}, u32[]{:S(2)}) collective-permute-start(bf16[128,576]{1,0:T(8,128)(2,1)S(1)} %collective-permute-done.10.refs_0_), channel_id=1, source_target_pairs={{0,2},{1,3},{2,0},{3,1},{4,6},{5,7},{6,4},{7,5},{8,10},{9,11},{10,... | collective-permute-start | bytes 442376 | tf_op jit(solution)/shard_map/ppermute | solution.py:337
  49.6 3.5 %order_query.1 = (bf16[3,512,512]{2,1,0:T(8,128)(2,1)S(1)}, bf16[3,512,512]{2,1,0:T(8,128)(2,1)S(1)}) custom-call(bf16[512,1536]{1,0:T(8,128)(2,1)S(1)} %bitcast.21), custom_call_target="tpu_custom_call" | custom-call | flops 2500000000 | bytes 6000000 | tf_op jit(solution)/shard_map/order_query/pallas_call | solution.py:290
  54.9 2.7 %collective-permute-start.14 = (bf16[32,4992]{1,0:T(8,128)(2,1)S(1)}, bf16[32,4992]{1,0:T(8,128)(2,1)S(1)}, u32[]{:S(2)}, u32[]{:S(2)}) collective-permute-start(bf16[32,4992]{1,0:T(8,128)(2,1)S(1)} %get-tuple-element.47), channel_id=1, source_target_pairs={{0,132},{4,0},{128,4},{132,128},{1,133},{5,1},{129,5},{133,129},{2... | collective-permute-start | bytes 958472 | tf_op jit(solution)/shard_map/ppermute | solution.py:337
  57.6 10.4 %collective-permute-start.18 = (bf16[64,4992]{1,0:T(8,128)(2,1)S(1)}, bf16[64,4992]{1,0:T(8,128)(2,1)S(1)}, u32[]{:S(2)}, u32[]{:S(2)}) collective-permute-start(bf16[64,4992]{1,0:T(8,128)(2,1)S(1)} %bitcast.15), channel_id=1, source_target_pairs={{0,64},{64,0},{1,65},{65,1},{2,66},{66,2},{3,67},{67,3},{4,68},{68... | collective-permute-start | bytes 1916936 | tf_op jit(solution)/shard_map/ppermute | solution.py:337
  68.5 1.9 %order_latent.1 = (bf16[1024,512]{1,0:T(8,128)(2,1)S(1)}, bf16[1024,512]{1,0:T(8,128)(2,1)S(1)}, bf16[1024,64]{1,0:T(8,128)(2,1)S(1)}) custom-call(s32[1]{0:T(128)} %bitcast.9.me_ref, bf16[512,512]{1,0:T(8,128)(2,1)S(1)} %bitcast.20, bf16[512,64]{1,0:T(8,128)(2,1)S(1)} %bitcast.18, bf16[128,576]{1,0:T(8,128)(2,1)S(1)} %collective-permute-done.10.refs_0_, ...), custom_call_target="tpu_custom_call" | custom-call | flops 1000000000 | bytes 4000000 | tf_op jit(solution)/shard_map/order_latent/pallas_call | solution.py:322
  71.4 1.5 %collective-permute-start.21 = (bf16[32,4992]{1,0:T(8,128)(2,1)S(1)}, bf16[32,4992]{1,0:T(8,128)(2,1)S(1)}, u32[]{:S(2)}, u32[]{:S(2)}) collective-permute-start(bf16[32,4992]{1,0:T(8,128)(2,1)S(1)} %collective-permute-done.13.rest_3_), channel_id=1, source_target_pairs={{0,64},{64,0},{1,65},{65,1},{2,66},{66,2},{3,67},{67,3},{4,68},{68... | collective-permute-start | bytes 958472 | tf_op jit(solution)/shard_map/ppermute | solution.py:337
  72.9 1.2 collective-permute-done.21.rest_8_
  74.6 11.8 %ringed.1 = (bf16[512,2048]{1,0:T(8,128)(2,1)}, f32[3,8,128]{2,1,0:T(8,128)S(1)}) custom-call(s32[3]{0:T(128)S(1)} %pad_add_fusion.place_ref, bf16[3,512,512]{2,1,0:T(8,128)(2,1)S(1)} %get-tuple-element.56.x_ref, bf16[1024,512]{1,0:T(8,128)(2,1)S(1)} %get-tuple-element.57.lat_ref, bf16[1024,64]{1,0:T(8,128)(2,1)S(1)} %get-tuple-element.54.rope_ref, ...), custom_call_target="tpu_custom_call" | custom-call | flops 5400000000 | bytes 6000000 | tf_op jit(solution)/shard_map/ringed/pallas_call | solution.py:158
  86.5 18.9 %gathered.1 = (bf16[512,2048]{1,0:T(8,128)(2,1)}, f32[5,8,128]{2,1,0:T(8,128)S(1)}) custom-call(s32[3]{0:T(128)S(1)} %pad_add_fusion.place_ref, bf16[3,512,512]{2,1,0:T(8,128)(2,1)} %copy-done.4, bf16[1024,512]{1,0:T(8,128)(2,1)} %copy-done.2, bf16[1024,64]{1,0:T(8,128)(2,1)} %copy-done.3, ...), custom_call_target="tpu_custom_call", output_to_operand_aliasing={{0}: (5, {})} | custom-call | flops 8999999488 | bytes 10000000 | tf_op jit(solution)/shard_map/gathered/pallas_call | solution.py:158
  105.6 14.9 %all_to_all.5 = f32[64,1,16]{2,1,0:T(1,128)S(1)} all-to-all(f32[64,1,16]{2,1,0:T(1,128)S(1)} %broadcast_in_dim.12), channel_id=1, replica_groups=mesh['xh'=2,'core'=2,'z'=8,'xl'=2,'tensor'=4] {'xh','core','z','xl'}, dimensions={0} | all-to-all | bytes 8192 | tf_op jit(solution)/shard_map/all_to_all | solution.py:389
  (70 shorter events, 10.5 us)
Async XLA Ops:
  7.2 79.3 %all-gather.2.cloned.1.call-start = ((), (), s32[]{:S(2)}) async-start(), calls=%async_computation.1 | async-start | bytes 9052160 | tf_op jit(solution)/shard_map/all_gather | solution.py:355
  8.3 6.1 %collective-permute-start.7 = (bf16[8,8320]{1,0:T(8,128)(2,1)S(1)}, bf16[8,8320]{1,0:T(8,128)(2,1)S(1)}, u32[]{:S(2)}, u32[]{:S(2)}) collective-permute-start(bf16[8,8320]{1,0:T(8,128)(2,1)S(1)} %get-tuple-element.35.refs_0_), channel_id=1, source_target_pairs={{0,4},{4,128},{128,132},{132,0},{1,5},{5,129},{129,133},{133,1},{2... | collective-permute-start | bytes 399368 | tf_op jit(solution)/shard_map/ppermute | solution.py:337
  10.4 4.0 %collective-permute-start.8 = (bf16[8,8320]{1,0:T(8,128)(2,1)S(1)}, bf16[8,8320]{1,0:T(8,128)(2,1)S(1)}, u32[]{:S(2)}, u32[]{:S(2)}) collective-permute-start(bf16[8,8320]{1,0:T(8,128)(2,1)S(1)} %get-tuple-element.35.refs_0_), channel_id=1, source_target_pairs={{0,132},{4,0},{128,4},{132,128},{1,133},{5,1},{129,5},{133,129},{2... | collective-permute-start | bytes 399368 | tf_op jit(solution)/shard_map/ppermute | solution.py:337
  11.8 6.4 %collective-permute-start.9 = (bf16[8,8320]{1,0:T(8,128)(2,1)S(1)}, bf16[8,8320]{1,0:T(8,128)(2,1)S(1)}, u32[]{:S(2)}, u32[]{:S(2)}) collective-permute-start(bf16[8,8320]{1,0:T(8,128)(2,1)S(1)} %get-tuple-element.35.refs_0_), channel_id=1, source_target_pairs={{0,128},{4,132},{128,0},{132,4},{1,129},{5,133},{129,1},{133,5},{2... | collective-permute-start | bytes 399368 | tf_op jit(solution)/shard_map/ppermute | solution.py:337
  19.0 9.1 %collective-permute-start.3 = (bf16[8,4992]{1,0:T(8,128)(2,1)S(1)}, bf16[8,4992]{1,0:T(8,128)(2,1)S(1)}, u32[]{:S(2)}, u32[]{:S(2)}) collective-permute-start(bf16[8,4992]{1,0:T(8,128)(2,1)S(1)} %get-tuple-element.34.refs_0_), channel_id=1, source_target_pairs={{0,48},{8,56},{16,0},{24,8},{32,16},{40,24},{48,32},{56,40},{1,49}... | collective-permute-start | bytes 239624 | tf_op jit(solution)/shard_map/ppermute | solution.py:337
  25.9 8.0 %collective-permute-start.2 = (bf16[8,4992]{1,0:T(8,128)(2,1)S(1)}, bf16[8,4992]{1,0:T(8,128)(2,1)S(1)}, u32[]{:S(2)}, u32[]{:S(2)}) collective-permute-start(bf16[8,4992]{1,0:T(8,128)(2,1)S(1)} %get-tuple-element.34.refs_0_), channel_id=1, source_target_pairs={{0,16},{8,24},{16,32},{24,40},{32,48},{40,56},{48,0},{56,8},{1,17}... | collective-permute-start | bytes 239624 | tf_op jit(solution)/shard_map/ppermute | solution.py:337
  28.1 7.7 %collective-permute-start.5 = (bf16[8,4992]{1,0:T(8,128)(2,1)S(1)}, bf16[8,4992]{1,0:T(8,128)(2,1)S(1)}, u32[]{:S(2)}, u32[]{:S(2)}) collective-permute-start(bf16[8,4992]{1,0:T(8,128)(2,1)S(1)} %collective-permute-done.3.refs_4_), channel_id=1, source_target_pairs={{0,56},{8,0},{16,8},{24,16},{32,24},{40,32},{48,40},{56,48},{1,57}... | collective-permute-start | bytes 239624 | tf_op jit(solution)/shard_map/ppermute | solution.py:337
  31.1 11.4 %collective-permute-start.10 = (bf16[128,576]{1,0:T(8,128)(2,1)S(1)}, bf16[128,576]{1,0:T(8,128)(2,1)S(1)}, u32[]{:S(2)}, u32[]{:S(2)}) collective-permute-start(bf16[128,576]{1,0:T(8,128)(2,1)S(1)} %pad_maximum_fusion), channel_id=1, source_target_pairs={{0,4},{4,8},{8,12},{12,16},{16,20},{20,24},{24,28},{28,32},{32,36}... | collective-permute-start | bytes 442376 | tf_op jit(solution)/shard_map/ppermute | solution.py:337
  31.2 7.5 %collective-permute-start = (bf16[8,4992]{1,0:T(8,128)(2,1)S(1)}, bf16[8,4992]{1,0:T(8,128)(2,1)S(1)}, u32[]{:S(2)}, u32[]{:S(2)}) collective-permute-start(bf16[8,4992]{1,0:T(8,128)(2,1)S(1)} %get-tuple-element.34.refs_0_), channel_id=1, source_target_pairs={{0,8},{8,16},{16,24},{24,32},{32,40},{40,48},{48,56},{56,0},{1,9},... | collective-permute-start | bytes 239624 | tf_op jit(solution)/shard_map/ppermute | solution.py:337
  31.3 7.4 %collective-permute-start.1 = (bf16[8,4992]{1,0:T(8,128)(2,1)S(1)}, bf16[8,4992]{1,0:T(8,128)(2,1)S(1)}, u32[]{:S(2)}, u32[]{:S(2)}) collective-permute-start(bf16[8,4992]{1,0:T(8,128)(2,1)S(1)} %get-tuple-element.34.refs_0_), channel_id=1, source_target_pairs={{0,56},{8,0},{16,8},{24,16},{32,24},{40,32},{48,40},{56,48},{1,57}... | collective-permute-start | bytes 239624 | tf_op jit(solution)/shard_map/ppermute | solution.py:337
  33.9 6.5 %collective-permute-start.4 = (bf16[8,4992]{1,0:T(8,128)(2,1)S(1)}, bf16[8,4992]{1,0:T(8,128)(2,1)S(1)}, u32[]{:S(2)}, u32[]{:S(2)}) collective-permute-start(bf16[8,4992]{1,0:T(8,128)(2,1)S(1)} %collective-permute-done.2.refs_3_), channel_id=1, source_target_pairs={{0,8},{8,16},{16,24},{24,32},{32,40},{40,48},{48,56},{56,0},{1,9},... | collective-permute-start | bytes 239624 | tf_op jit(solution)/shard_map/ppermute | solution.py:337
  35.8 6.6 %collective-permute-start.6 = (bf16[8,4992]{1,0:T(8,128)(2,1)S(1)}, bf16[8,4992]{1,0:T(8,128)(2,1)S(1)}, u32[]{:S(2)}, u32[]{:S(2)}) collective-permute-start(bf16[8,4992]{1,0:T(8,128)(2,1)S(1)} %collective-permute-done.5.refs_6_), channel_id=1, source_target_pairs={{0,56},{8,0},{16,8},{24,16},{32,24},{40,32},{48,40},{56,48},{1,57}... | collective-permute-start | bytes 239624 | tf_op jit(solution)/shard_map/ppermute | solution.py:337
  42.5 12.3 %collective-permute-start.11 = (bf16[64,4992]{1,0:T(8,128)(2,1)S(1)}, bf16[64,4992]{1,0:T(8,128)(2,1)S(1)}, u32[]{:S(2)}, u32[]{:S(2)}) collective-permute-start(bf16[64,4992]{1,0:T(8,128)(2,1)S(1)} %bitcast.13), channel_id=1, source_target_pairs={{0,4},{4,128},{128,132},{132,0},{1,5},{5,129},{129,133},{133,1},{2... | collective-permute-start | bytes 1916936 | tf_op jit(solution)/shard_map/ppermute | solution.py:337
  43.4 11.4 %collective-permute-start.12 = (bf16[64,4992]{1,0:T(8,128)(2,1)S(1)}, bf16[64,4992]{1,0:T(8,128)(2,1)S(1)}, u32[]{:S(2)}, u32[]{:S(2)}) collective-permute-start(bf16[64,4992]{1,0:T(8,128)(2,1)S(1)} %bitcast.14), channel_id=1, source_target_pairs={{0,132},{4,0},{128,4},{132,128},{1,133},{5,1},{129,5},{133,129},{2... | collective-permute-start | bytes 1916936 | tf_op jit(solution)/shard_map/ppermute | solution.py:337
  45.3 12.3 %collective-permute-start.15 = (bf16[128,576]{1,0:T(8,128)(2,1)S(1)}, bf16[128,576]{1,0:T(8,128)(2,1)S(1)}, u32[]{:S(2)}, u32[]{:S(2)}) collective-permute-start(bf16[128,576]{1,0:T(8,128)(2,1)S(1)} %collective-permute-done.10.refs_0_), channel_id=1, source_target_pairs={{0,1},{1,2},{2,3},{3,0},{4,5},{5,6},{6,7},{7,4},{8,9},{9,10},{10,1... | collective-permute-start | bytes 442376 | tf_op jit(solution)/shard_map/ppermute | solution.py:337
  46.5 21.5 %collective-permute-start.16 = (bf16[128,576]{1,0:T(8,128)(2,1)S(1)}, bf16[128,576]{1,0:T(8,128)(2,1)S(1)}, u32[]{:S(2)}, u32[]{:S(2)}) collective-permute-start(bf16[128,576]{1,0:T(8,128)(2,1)S(1)} %collective-permute-done.10.refs_0_), channel_id=1, source_target_pairs={{0,3},{1,0},{2,1},{3,2},{4,7},{5,4},{6,5},{7,6},{8,11},{9,8},{10,9... | collective-permute-start | bytes 442376 | tf_op jit(solution)/shard_map/ppermute | solution.py:337
  47.9 20.1 %collective-permute-start.17 = (bf16[128,576]{1,0:T(8,128)(2,1)S(1)}, bf16[128,576]{1,0:T(8,128)(2,1)S(1)}, u32[]{:S(2)}, u32[]{:S(2)}) collective-permute-start(bf16[128,576]{1,0:T(8,128)(2,1)S(1)} %collective-permute-done.10.refs_0_), channel_id=1, source_target_pairs={{0,2},{1,3},{2,0},{3,1},{4,6},{5,7},{6,4},{7,5},{8,10},{9,11},{10,... | collective-permute-start | bytes 442376 | tf_op jit(solution)/shard_map/ppermute | solution.py:337
  54.8 16.6 %collective-permute-start.13 = (bf16[32,4992]{1,0:T(8,128)(2,1)S(1)}, bf16[32,4992]{1,0:T(8,128)(2,1)S(1)}, u32[]{:S(2)}, u32[]{:S(2)}) collective-permute-start(bf16[32,4992]{1,0:T(8,128)(2,1)S(1)} %get-tuple-element.46), channel_id=1, source_target_pairs={{0,4},{4,128},{128,132},{132,0},{1,5},{5,129},{129,133},{133,1},{2... | collective-permute-start | bytes 958472 | tf_op jit(solution)/shard_map/ppermute | solution.py:337
  54.9 16.5 %collective-permute-start.14 = (bf16[32,4992]{1,0:T(8,128)(2,1)S(1)}, bf16[32,4992]{1,0:T(8,128)(2,1)S(1)}, u32[]{:S(2)}, u32[]{:S(2)}) collective-permute-start(bf16[32,4992]{1,0:T(8,128)(2,1)S(1)} %get-tuple-element.47), channel_id=1, source_target_pairs={{0,132},{4,0},{128,4},{132,128},{1,133},{5,1},{129,5},{133,129},{2... | collective-permute-start | bytes 958472 | tf_op jit(solution)/shard_map/ppermute | solution.py:337
  57.6 15.4 %collective-permute-start.18 = (bf16[64,4992]{1,0:T(8,128)(2,1)S(1)}, bf16[64,4992]{1,0:T(8,128)(2,1)S(1)}, u32[]{:S(2)}, u32[]{:S(2)}) collective-permute-start(bf16[64,4992]{1,0:T(8,128)(2,1)S(1)} %bitcast.15), channel_id=1, source_target_pairs={{0,64},{64,0},{1,65},{65,1},{2,66},{66,2},{3,67},{67,3},{4,68},{68... | collective-permute-start | bytes 1916936 | tf_op jit(solution)/shard_map/ppermute | solution.py:337
  68.0 6.7 %collective-permute-start.19 = (bf16[64,4992]{1,0:T(8,128)(2,1)S(1)}, bf16[64,4992]{1,0:T(8,128)(2,1)S(1)}, u32[]{:S(2)}, u32[]{:S(2)}) collective-permute-start(bf16[64,4992]{1,0:T(8,128)(2,1)S(1)} %collective-permute-done.11.before_ref.rest_1_), channel_id=1, source_target_pairs={{0,64},{64,0},{1,65},{65,1},{2,66},{66,2},{3,67},{67,3},{4,68},{68... | collective-permute-start | bytes 1916936 | tf_op jit(solution)/shard_map/ppermute | solution.py:337
  68.1 6.6 %collective-permute-start.20 = (bf16[64,4992]{1,0:T(8,128)(2,1)S(1)}, bf16[64,4992]{1,0:T(8,128)(2,1)S(1)}, u32[]{:S(2)}, u32[]{:S(2)}) collective-permute-start(bf16[64,4992]{1,0:T(8,128)(2,1)S(1)} %collective-permute-done.12.after_ref.rest_2_), channel_id=1, source_target_pairs={{0,64},{64,0},{1,65},{65,1},{2,66},{66,2},{3,67},{67,3},{4,68},{68... | collective-permute-start | bytes 1916936 | tf_op jit(solution)/shard_map/ppermute | solution.py:337
  71.4 2.8 %collective-permute-start.21 = (bf16[32,4992]{1,0:T(8,128)(2,1)S(1)}, bf16[32,4992]{1,0:T(8,128)(2,1)S(1)}, u32[]{:S(2)}, u32[]{:S(2)}) collective-permute-start(bf16[32,4992]{1,0:T(8,128)(2,1)S(1)} %collective-permute-done.13.rest_3_), channel_id=1, source_target_pairs={{0,64},{64,0},{1,65},{65,1},{2,66},{66,2},{3,67},{67,3},{4,68},{68... | collective-permute-start | bytes 958472 | tf_op jit(solution)/shard_map/ppermute | solution.py:337
  72.9 1.7 %collective-permute-start.22 = (bf16[32,4992]{1,0:T(8,128)(2,1)S(1)}, bf16[32,4992]{1,0:T(8,128)(2,1)S(1)}, u32[]{:S(2)}, u32[]{:S(2)}) collective-permute-start(bf16[32,4992]{1,0:T(8,128)(2,1)S(1)} %collective-permute-done.14.rest_4_), channel_id=1, source_target_pairs={{0,64},{64,0},{1,65},{65,1},{2,66},{66,2},{3,67},{67,3},{4,68},{68... | collective-permute-start | bytes 958472 | tf_op jit(solution)/shard_map/ppermute | solution.py:337
  (9 other events, 181.5 us)
Sparse Core Ops, SparseCore 0:
  19.2 62.8 all-gather.1
